TPU v7x, 32 devices: a whole 2x2x4 slice. The times are simulated.
32 devices in a mesh: grp: 4 (over y, core), site: 8 (over z, x).
Axes of the slice: x: 2, y: 2, z: 4, core: 2. Of those that a mesh axis runs over, the one named last changes fastest.
Arguments:
- noise: bfloat16 [64, 4096], P(('grp', 'site')), may hold values from -25 to 25, as said below
- sites: bfloat16 [4096, 4096], P('site'), may hold values from -25 to 25, as said below
- weights: float32 [4096], P('site'), may hold values from -2 to 2
Outputs:
- targets: bfloat16 [64, 4096], P(('grp', 'site'))
- potentials: float32 [64], P(('grp', 'site'))
- new_weights: float32 [4096], P('site')
Inputs may be any that keep to these rules, and one draw needn't show every extreme that they name: Entries of the noise rows are finite reals. Entries of the sites are finite reals.
All inputs are finite; a program needn't handle non-finite values.
Results may differ from a plain program's by a relative error of at most 0.014.
Values may be sent and summed in bfloat16 or wider, within the bound.
A program may use at most 64 MiB of HBM per device.

v0:
```python
import functools
import math

import jax
import jax.numpy as jnp
from jax import lax
from jax.experimental import pallas as pl
from jax.experimental.pallas import tpu as pltpu
from jax.sharding import PartitionSpec as P

EPS = 0.006
ETA = 0.05
MESH = pl.DeviceIdType.MESH
F32 = jnp.float32
BF16 = jnp.bfloat16


def steps(count, body):
    if count <= 16:
        for k in range(count):
            body(k)
    else:
        lax.fori_loop(0, count, lambda k, c: (body(k), c)[1], 0)


def kernel(n, g, noise_ref, sites_ref, weights_ref, tgt_ref, pot_ref, neww_ref,
           sites_v, weights_v, noise_all, noise_f, sq_acc, t_send, t_all,
           stat_send, stat_all, mass_send, mass_all,
           site_sem, own_sem, ns_sem, nr_sem, ts_sem, tr_sem, ss_sem, sr_sem, ms_sem, mr_sem):
    me = lax.axis_index("site")
    mg = lax.axis_index("grp")
    rows_dev, width = noise_ref.shape
    n_loc = sites_ref.shape[0]
    rows = rows_dev * n
    lanes = stat_send.shape[1]
    chunks = site_sem.shape[0]
    crow = n_loc // chunks
    parts, wide = t_send.shape[0], t_send.shape[3]

    def site_copy(c):
        part = pl.ds(c * crow, crow)
        return pltpu.make_async_copy(sites_ref.at[part, :], sites_v.at[part, :], site_sem.at[c])

    barrier = pltpu.get_barrier_semaphore()

    def greet_site(k):
        pl.semaphore_signal(barrier, inc=1, device_id={"site": lax.rem(me + k + 1, n)}, device_id_type=MESH)

    def greet_grp(k):
        pl.semaphore_signal(barrier, inc=1, device_id={"grp": lax.rem(mg + k + 1, g)}, device_id_type=MESH)

    steps(n - 1, greet_site)
    steps(g - 1, greet_grp)
    for c in range(chunks):
        site_copy(c).start()
    for c in range(parts):
        pltpu.make_async_copy(noise_ref.at[:, pl.ds(c * wide, wide)], noise_all.at[c, me], own_sem.at[0]).start()
    own_w = pltpu.make_async_copy(weights_ref, weights_v, own_sem.at[1])
    own_w.start()
    pl.semaphore_wait(barrier, n + g - 2)

    def to_site(src, dst, s_sem, r_sem, t):
        pltpu.make_async_remote_copy(
            src_ref=src, dst_ref=dst, send_sem=s_sem, recv_sem=r_sem,
            device_id={"site": t}, device_id_type=MESH).start()

    def drain(blocks, sem):
        pltpu.make_async_copy(blocks, blocks, sem).wait()

    def other(k):
        return lax.rem(me + k + 1, n)

    for c in range(parts):
        steps(n - 1, lambda k: to_site(noise_ref.at[:, pl.ds(c * wide, wide)], noise_all.at[c, me],
                                       ns_sem.at[c], nr_sem.at[c], other(k)))

    for c in range(chunks):
        site_copy(c).wait()
        acc = None
        for j in range(width // 128):
            x = sites_v[c * crow:(c + 1) * crow, j * 128:(j + 1) * 128].astype(F32)
            acc = x * x if acc is None else acc + x * x
        sq_acc[c * crow:(c + 1) * crow, :] = acc
    half_sq = jnp.sum(sq_acc[...].T, axis=0, keepdims=True) / (2.0 * width)
    drain(noise_ref, own_sem.at[0])
    own_w.wait()
    own_sq = 0.0
    for c in range(parts):
        mine = noise_all[c, me].astype(F32)
        own_sq = own_sq + jnp.sum(mine * mine, axis=1, keepdims=True)
    own_sq = own_sq / (2.0 * width)

    inner = None
    for c in range(parts):
        drain(noise_all.at[c, pl.ds(0, n - 1)], nr_sem.at[c])
        for d in range(n):
            noise_f[c, d * rows_dev:(d + 1) * rows_dev, :] = noise_all[c, d].astype(F32)
        term = lax.dot_general(noise_f[c].astype(BF16), sites_v[:, c * wide:(c + 1) * wide],
                               (((1,), (1,)), ((), ())), preferred_element_type=F32)
        inner = term if inner is None else inner + term
    score = weights_v[...] + (inner / width - half_sq) / EPS
    top = jnp.max(score, axis=1, keepdims=True)
    shifted = jnp.exp(score - top)
    total = jnp.sum(shifted, axis=1, keepdims=True)
    lse_d = top + jnp.log(total)

    diag = (lax.broadcasted_iota(jnp.int32, (rows, lanes), 0)
            == lax.broadcasted_iota(jnp.int32, (rows, lanes), 1))
    stat_send[...] = jnp.sum(jnp.where(diag, lse_d, 0.0), axis=0, keepdims=True)
    steps(n - 1, lambda k: to_site(stat_send, stat_all.at[me], ss_sem, sr_sem, other(k)))
    stat_all[me] = stat_send[...]

    probs = shifted.astype(BF16)
    inv = 1.0 / total
    for c in range(parts):
        part = jnp.dot(probs, sites_v[:, c * wide:(c + 1) * wide], preferred_element_type=F32) * inv
        for d in range(n):
            t_send[c, d] = part[d * rows_dev:(d + 1) * rows_dev, :].astype(BF16)

        def t_to(k):
            t = other(k)
            to_site(t_send.at[c, t], t_all.at[c, me], ts_sem.at[c], tr_sem.at[c], t)

        steps(n - 1, t_to)

    drain(stat_all.at[pl.ds(0, n - 1)], sr_sem)
    stats = stat_all[...]
    peak = jnp.max(stats, axis=0)
    lse_row = peak + jnp.log(jnp.sum(jnp.exp(stats - peak[None]), axis=0))
    lse = jnp.sum(jnp.where(diag, lse_row, 0.0), axis=1, keepdims=True)
    mass_part = jnp.sum(jnp.exp(score - lse), axis=0, keepdims=True)
    mass_send[...] = mass_part

    def mass_to(k):
        pltpu.make_async_remote_copy(
            src_ref=mass_send, dst_ref=mass_all.at[mg], send_sem=ms_sem, recv_sem=mr_sem,
            device_id={"grp": lax.rem(mg + k + 1, g)}, device_id_type=MESH).start()

    steps(g - 1, mass_to)
    mass_all[mg] = mass_part

    mine_diag = (lax.broadcasted_iota(jnp.int32, (rows_dev, lanes), 0) + me * rows_dev
                 == lax.broadcasted_iota(jnp.int32, (rows_dev, lanes), 1))
    own_lse = jnp.sum(jnp.where(mine_diag, lse_row, 0.0), axis=1, keepdims=True)
    pot = own_sq - EPS * (own_lse - math.log(float(n_loc * n)))
    first = (lax.broadcasted_iota(jnp.int32, (rows_dev, 128), 0)
             == lax.broadcasted_iota(jnp.int32, (rows_dev, 128), 1))
    pot_ref[...] = jnp.sum(jnp.where(first, pot, 0.0), axis=0, keepdims=True)[:, :rows_dev]

    shares = []
    for d in range(n):
        share_row = jnp.exp(stat_all[d] - lse_row)
        shares.append(jnp.sum(jnp.where(mine_diag, share_row, 0.0), axis=1, keepdims=True))
    for c in range(parts):
        t_all[c, me] = t_send[c, me]
    for c in range(parts):
        drain(t_all.at[c, pl.ds(0, n - 1)], tr_sem.at[c])
        acc = None
        for d in range(n):
            term = shares[d] * t_all[c, d].astype(F32)
            acc = term if acc is None else acc + term
        tgt_ref[:, c * wide:(c + 1) * wide] = acc.astype(BF16)

    drain(mass_all.at[pl.ds(0, g - 1)], mr_sem)
    mass = jnp.sum(mass_all[...], axis=0)
    neww_ref[...] = weights_v[...] + ETA * (1.0 - float(n_loc * n) / float(rows * g) * mass)

    drain(stat_all.at[pl.ds(0, n - 1)], ss_sem)
    for c in range(parts):
        drain(noise_all.at[c, pl.ds(0, n - 1)], ns_sem.at[c])
        drain(t_all.at[c, pl.ds(0, n - 1)], ts_sem.at[c])
    drain(mass_all.at[pl.ds(0, g - 1)], ms_sem)


def place(tgt, pot, neww, tgt_out, pot_out, neww_out, sems):
    copies = [pltpu.make_async_copy(src, dst, sems.at[i])
              for i, (src, dst) in enumerate(((tgt, tgt_out), (pot, pot_out), (neww, neww_out)))]
    for copy in copies:
        copy.start()
    for copy in copies:
        copy.wait()


def shards(n, g, noise, sites, weights):
    rows_dev, width = noise.shape
    n_loc = sites.shape[0]
    rows = rows_dev * n
    lanes = max(128, rows)
    chunks, parts = 8, 4
    vmem = pl.BlockSpec(memory_space=pltpu.VMEM)
    anym = pl.BlockSpec(memory_space=pl.ANY)
    dma = pltpu.SemaphoreType.DMA
    tgt, pot, neww = pl.pallas_call(
        functools.partial(kernel, n, g),
        out_shape=(
            pltpu.VMEM((rows_dev, width), BF16),
            pltpu.VMEM((1, rows_dev), F32),
            pltpu.VMEM((1, n_loc), F32),
        ),
        in_specs=[anym, anym, anym],
        out_specs=(vmem, vmem, vmem),
        scratch_shapes=[
            pltpu.VMEM((n_loc, width), BF16),
            pltpu.VMEM((1, n_loc), F32),
            pltpu.VMEM((parts, n, rows_dev, width // parts), BF16),
            pltpu.VMEM((parts, rows, width // parts), F32),
            pltpu.VMEM((n_loc, 128), F32),
            pltpu.VMEM((parts, n, rows_dev, width // parts), BF16),
            pltpu.VMEM((parts, n, rows_dev, width // parts), BF16),
            pltpu.VMEM((1, lanes), F32),
            pltpu.VMEM((n, 1, lanes), F32),
            pltpu.VMEM((1, n_loc), F32),
            pltpu.VMEM((g, 1, n_loc), F32),
            dma((chunks,)), dma((2,)), dma((parts,)), dma((parts,)), dma((parts,)), dma((parts,)),
            dma(()), dma(()), dma(()), dma(()),
        ],
        compiler_params=pltpu.CompilerParams(
            collective_id=0, has_side_effects=True, vmem_limit_bytes=56 * 1024 * 1024),
        name="dual_step",
    )(noise, sites, weights.reshape(1, n_loc))
    outs = (tgt, pot.reshape(rows_dev), neww.reshape(n_loc))
    return pl.pallas_call(
        place,
        out_shape=tuple(jax.ShapeDtypeStruct(o.shape, o.dtype) for o in outs),
        in_specs=[vmem] * 3,
        out_specs=(anym,) * 3,
        scratch_shapes=[dma((3,))],
        compiler_params=pltpu.CompilerParams(vmem_limit_bytes=1024 * 1024),
        name="place",
    )(*outs)


def solution(mesh):
    n, g = mesh.shape["site"], mesh.shape["grp"]
    in_specs = (P(("grp", "site"), None), P("site", None), P("site"))
    out_specs = (P(("grp", "site"), None), P(("grp", "site")), P("site"))
    return jax.shard_map(functools.partial(shards, n, g), mesh=mesh, in_specs=in_specs,
                         out_specs=out_specs, check_vma=False)
```

profile of v0, /device:TPU:0, one launch (start us, length us, event | category | flops | bytes accessed | tf_op | source)
XLA Modules:
  0.0 20.8 jit_solution(753896997892171253)
XLA Ops:
  0.6 19.5 %dual_step.1 = (bf16[2,4096]{1,0:T(2,128)(2,1)S(1)}, f32[1,2]{1,0:T(1,128)S(1)}, f32[1,512]{1,0:T(1,128)S(1)}) custom-call(bf16[2,4096]{1,0:T(2,128)(2,1)} %noise_ref.1, bf16[512,4096]{1,0:T(8,128)(2,1)} %sites_ref.1, f32[1,512]{1,0:T(1,128)} %bitcast.5), custom_call_target="tpu_custom_call" | custom-call | tf_op jit(solution)/shard_map/dual_step/pallas_call | solution.py:193
  20.1 0.6 %place.1 = (bf16[2,4096]{1,0:T(2,128)(2,1)}, f32[2]{0:T(128)}, f32[512]{0:T(512)}) custom-call(bf16[2,4096]{1,0:T(2,128)(2,1)S(1)} %get-tuple-element.6.tgt, f32[2]{0:T(128)S(1)} %bitcast.4, f32[512]{0:T(512)S(1)} %bitcast.3), custom_call_target="tpu_custom_call" | custom-call | tf_op jit(solution)/shard_map/place/pallas_call | solution.py:222
where the time goes:
time: 20.9 us; the launch traced here: 20.8 us
  Pallas kernels  20.1 us (96%)
  between operations  0.64 us (3%)
    pallas_call x1, Pallas kernels, shards(): pl.pallas_call(functools.partial(kernel, n, g), out_shape=(pltpu.VMEM((ro...  19.5 us
    pallas_call x1, Pallas kernels, shards(): pl.pallas_call(place, out_shape=tuple((jax.ShapeDtypeStruct(o.shape, o.dt...  0.64 us

commit v1 on v0

--- a/solution.py
+++ b/solution.py
@@ -70,17 +70,27 @@
     def other(k):
         return lax.rem(me + k + 1, n)
 
-    for c in range(parts):
-        steps(n - 1, lambda k: to_site(noise_ref.at[:, pl.ds(c * wide, wide)], noise_all.at[c, me],
+    def columns(c):
+        return pl.ds(pl.multiple_of(c * wide, wide), wide)
+
+    def noise_to(c, carry):
+        steps(n - 1, lambda k: to_site(noise_ref.at[:, columns(c)], noise_all.at[c, me],
                                        ns_sem.at[c], nr_sem.at[c], other(k)))
-
-    for c in range(chunks):
+        return carry
+
+    lax.fori_loop(0, parts, noise_to, 0)
+
+    def squares(c, carry):
         site_copy(c).wait()
+        part = pl.ds(pl.multiple_of(c * crow, crow), crow)
         acc = None
         for j in range(width // 128):
-            x = sites_v[c * crow:(c + 1) * crow, j * 128:(j + 1) * 128].astype(F32)
+            x = sites_v[part, j * 128:(j + 1) * 128].astype(F32)
             acc = x * x if acc is None else acc + x * x
-        sq_acc[c * crow:(c + 1) * crow, :] = acc
+        sq_acc[part, :] = acc
+        return carry
+
+    lax.fori_loop(0, chunks, squares, 0)
     half_sq = jnp.sum(sq_acc[...].T, axis=0, keepdims=True) / (2.0 * width)
     drain(noise_ref, own_sem.at[0])
     own_w.wait()
@@ -90,14 +100,14 @@
         own_sq = own_sq + jnp.sum(mine * mine, axis=1, keepdims=True)
     own_sq = own_sq / (2.0 * width)
 
-    inner = None
-    for c in range(parts):
+    def inner_part(c, inner):
         drain(noise_all.at[c, pl.ds(0, n - 1)], nr_sem.at[c])
         for d in range(n):
-            noise_f[c, d * rows_dev:(d + 1) * rows_dev, :] = noise_all[c, d].astype(F32)
-        term = lax.dot_general(noise_f[c].astype(BF16), sites_v[:, c * wide:(c + 1) * wide],
-                               (((1,), (1,)), ((), ())), preferred_element_type=F32)
-        inner = term if inner is None else inner + term
+            noise_f[d * rows_dev:(d + 1) * rows_dev, :] = noise_all[c, d].astype(F32)
+        return inner + lax.dot_general(noise_f[...].astype(BF16), sites_v[:, columns(c)],
+                                       (((1,), (1,)), ((), ())), preferred_element_type=F32)
+
+    inner = lax.fori_loop(0, parts, inner_part, jnp.zeros((rows, n_loc), F32))
     score = weights_v[...] + (inner / width - half_sq) / EPS
     top = jnp.max(score, axis=1, keepdims=True)
     shifted = jnp.exp(score - top)
@@ -112,8 +122,8 @@
 
     probs = shifted.astype(BF16)
     inv = 1.0 / total
-    for c in range(parts):
-        part = jnp.dot(probs, sites_v[:, c * wide:(c + 1) * wide], preferred_element_type=F32) * inv
+    def targets(c, carry):
+        part = jnp.dot(probs, sites_v[:, columns(c)], preferred_element_type=F32) * inv
         for d in range(n):
             t_send[c, d] = part[d * rows_dev:(d + 1) * rows_dev, :].astype(BF16)
 
@@ -122,6 +132,9 @@
             to_site(t_send.at[c, t], t_all.at[c, me], ts_sem.at[c], tr_sem.at[c], t)
 
         steps(n - 1, t_to)
+        return carry
+
+    lax.fori_loop(0, parts, targets, 0)
 
     drain(stat_all.at[pl.ds(0, n - 1)], sr_sem)
     stats = stat_all[...]
@@ -153,13 +166,16 @@
         shares.append(jnp.sum(jnp.where(mine_diag, share_row, 0.0), axis=1, keepdims=True))
     for c in range(parts):
         t_all[c, me] = t_send[c, me]
-    for c in range(parts):
+    def combine(c, carry):
         drain(t_all.at[c, pl.ds(0, n - 1)], tr_sem.at[c])
         acc = None
         for d in range(n):
             term = shares[d] * t_all[c, d].astype(F32)
             acc = term if acc is None else acc + term
-        tgt_ref[:, c * wide:(c + 1) * wide] = acc.astype(BF16)
+        tgt_ref[:, columns(c)] = acc.astype(BF16)
+        return carry
+
+    lax.fori_loop(0, parts, combine, 0)
 
     drain(mass_all.at[pl.ds(0, g - 1)], mr_sem)
     mass = jnp.sum(mass_all[...], axis=0)
@@ -203,7 +219,7 @@
             pltpu.VMEM((n_loc, width), BF16),
             pltpu.VMEM((1, n_loc), F32),
             pltpu.VMEM((parts, n, rows_dev, width // parts), BF16),
-            pltpu.VMEM((parts, rows, width // parts), F32),
+            pltpu.VMEM((rows, width // parts), F32),
             pltpu.VMEM((n_loc, 128), F32),
             pltpu.VMEM((parts, n, rows_dev, width // parts), BF16),
             pltpu.VMEM((parts, n, rows_dev, width // parts), BF16),

time: 20.9 us -> 21 us (level)
  no operation moved by 1% of the time
where the time goes in v1:
time: 21 us; the launch traced here: 20.9 us
  Pallas kernels  20.2 us (96%)
  between operations  0.64 us (3%)
    pallas_call x1, Pallas kernels, shards(): pl.pallas_call(functools.partial(kernel, n, g), out_shape=(pltpu.VMEM((ro...  19.6 us
    pallas_call x1, Pallas kernels, shards(): pl.pallas_call(place, out_shape=tuple((jax.ShapeDtypeStruct(o.shape, o.dt...  0.64 us

profile of v1, /device:TPU:0, one launch (start us, length us, event | category | flops | bytes accessed | tf_op | source)
XLA Modules:
  0.0 20.9 jit_solution(4479203043817379146)
XLA Ops:
  0.6 19.6 %dual_step.1 = (bf16[2,4096]{1,0:T(2,128)(2,1)S(1)}, f32[1,2]{1,0:T(1,128)S(1)}, f32[1,512]{1,0:T(1,128)S(1)}) custom-call(bf16[2,4096]{1,0:T(2,128)(2,1)} %noise_ref.1, bf16[512,4096]{1,0:T(8,128)(2,1)} %sites_ref.1, f32[1,512]{1,0:T(1,128)} %bitcast.5), custom_call_target="tpu_custom_call" | custom-call | tf_op jit(solution)/shard_map/dual_step/pallas_call | solution.py:209
  20.2 0.6 %place.1 = (bf16[2,4096]{1,0:T(2,128)(2,1)}, f32[2]{0:T(128)}, f32[512]{0:T(512)}) custom-call(bf16[2,4096]{1,0:T(2,128)(2,1)S(1)} %get-tuple-element.6.tgt, f32[2]{0:T(128)S(1)} %bitcast.4, f32[512]{0:T(512)S(1)} %bitcast.3), custom_call_target="tpu_custom_call" | custom-call | tf_op jit(solution)/shard_map/place/pallas_call | solution.py:238

commit v2 on v0

--- a/solution.py
+++ b/solution.py
@@ -36,6 +36,7 @@
     chunks = site_sem.shape[0]
     crow = n_loc // chunks
     parts, wide = t_send.shape[0], t_send.shape[3]
+    n_parts, n_wide = noise_all.shape[0], noise_all.shape[3]
 
     def site_copy(c):
         part = pl.ds(c * crow, crow)
@@ -53,10 +54,6 @@
     steps(g - 1, greet_grp)
     for c in range(chunks):
         site_copy(c).start()
-    for c in range(parts):
-        pltpu.make_async_copy(noise_ref.at[:, pl.ds(c * wide, wide)], noise_all.at[c, me], own_sem.at[0]).start()
-    own_w = pltpu.make_async_copy(weights_ref, weights_v, own_sem.at[1])
-    own_w.start()
     pl.semaphore_wait(barrier, n + g - 2)
 
     def to_site(src, dst, s_sem, r_sem, t):
@@ -70,9 +67,13 @@
     def other(k):
         return lax.rem(me + k + 1, n)
 
-    for c in range(parts):
-        steps(n - 1, lambda k: to_site(noise_ref.at[:, pl.ds(c * wide, wide)], noise_all.at[c, me],
+    for c in range(n_parts):
+        steps(n - 1, lambda k: to_site(noise_ref.at[:, pl.ds(c * n_wide, n_wide)], noise_all.at[c, me],
                                        ns_sem.at[c], nr_sem.at[c], other(k)))
+    for c in range(n_parts):
+        pltpu.make_async_copy(noise_ref.at[:, pl.ds(c * n_wide, n_wide)], noise_all.at[c, me], own_sem.at[0]).start()
+    own_w = pltpu.make_async_copy(weights_ref, weights_v, own_sem.at[1])
+    own_w.start()
 
     for c in range(chunks):
         site_copy(c).wait()
@@ -85,35 +86,31 @@
     drain(noise_ref, own_sem.at[0])
     own_w.wait()
     own_sq = 0.0
-    for c in range(parts):
+    for c in range(n_parts):
         mine = noise_all[c, me].astype(F32)
         own_sq = own_sq + jnp.sum(mine * mine, axis=1, keepdims=True)
     own_sq = own_sq / (2.0 * width)
 
     inner = None
-    for c in range(parts):
+    for c in range(n_parts):
         drain(noise_all.at[c, pl.ds(0, n - 1)], nr_sem.at[c])
         for d in range(n):
             noise_f[c, d * rows_dev:(d + 1) * rows_dev, :] = noise_all[c, d].astype(F32)
-        term = lax.dot_general(noise_f[c].astype(BF16), sites_v[:, c * wide:(c + 1) * wide],
+        term = lax.dot_general(noise_f[c].astype(BF16), sites_v[:, c * n_wide:(c + 1) * n_wide],
                                (((1,), (1,)), ((), ())), preferred_element_type=F32)
         inner = term if inner is None else inner + term
     score = weights_v[...] + (inner / width - half_sq) / EPS
     top = jnp.max(score, axis=1, keepdims=True)
     shifted = jnp.exp(score - top)
-    total = jnp.sum(shifted, axis=1, keepdims=True)
-    lse_d = top + jnp.log(total)
-
+    probs = shifted.astype(BF16)
     diag = (lax.broadcasted_iota(jnp.int32, (rows, lanes), 0)
             == lax.broadcasted_iota(jnp.int32, (rows, lanes), 1))
-    stat_send[...] = jnp.sum(jnp.where(diag, lse_d, 0.0), axis=0, keepdims=True)
-    steps(n - 1, lambda k: to_site(stat_send, stat_all.at[me], ss_sem, sr_sem, other(k)))
-    stat_all[me] = stat_send[...]
-
-    probs = shifted.astype(BF16)
-    inv = 1.0 / total
-    for c in range(parts):
-        part = jnp.dot(probs, sites_v[:, c * wide:(c + 1) * wide], preferred_element_type=F32) * inv
+
+    def as_row(column):
+        return jnp.sum(jnp.where(diag, column, 0.0), axis=0, keepdims=True)
+
+    for c in range(parts):
+        part = jnp.dot(probs, sites_v[:, c * wide:(c + 1) * wide], preferred_element_type=F32)
         for d in range(n):
             t_send[c, d] = part[d * rows_dev:(d + 1) * rows_dev, :].astype(BF16)
 
@@ -122,11 +119,20 @@
             to_site(t_send.at[c, t], t_all.at[c, me], ts_sem.at[c], tr_sem.at[c], t)
 
         steps(n - 1, t_to)
+        if c == 0:
+            stat_send[0:1, :] = as_row(top)
+            stat_send[1:2, :] = as_row(jnp.sum(shifted, axis=1, keepdims=True))
+            steps(n - 1, lambda k: to_site(stat_send, stat_all.at[me], ss_sem, sr_sem, other(k)))
+            stat_all[me] = stat_send[...]
 
     drain(stat_all.at[pl.ds(0, n - 1)], sr_sem)
-    stats = stat_all[...]
-    peak = jnp.max(stats, axis=0)
-    lse_row = peak + jnp.log(jnp.sum(jnp.exp(stats - peak[None]), axis=0))
+    peak = stat_all[0, 0:1, :]
+    for d in range(1, n):
+        peak = jnp.maximum(peak, stat_all[d, 0:1, :])
+    whole = 0.0
+    for d in range(n):
+        whole = whole + jnp.exp(stat_all[d, 0:1, :] - peak) * stat_all[d, 1:2, :]
+    lse_row = peak + jnp.log(jnp.where(whole > 0.0, whole, 1.0))
     lse = jnp.sum(jnp.where(diag, lse_row, 0.0), axis=1, keepdims=True)
     mass_part = jnp.sum(jnp.exp(score - lse), axis=0, keepdims=True)
     mass_send[...] = mass_part
@@ -149,7 +155,7 @@
 
     shares = []
     for d in range(n):
-        share_row = jnp.exp(stat_all[d] - lse_row)
+        share_row = jnp.exp(stat_all[d, 0:1, :] - lse_row)
         shares.append(jnp.sum(jnp.where(mine_diag, share_row, 0.0), axis=1, keepdims=True))
     for c in range(parts):
         t_all[c, me] = t_send[c, me]
@@ -166,8 +172,9 @@
     neww_ref[...] = weights_v[...] + ETA * (1.0 - float(n_loc * n) / float(rows * g) * mass)
 
     drain(stat_all.at[pl.ds(0, n - 1)], ss_sem)
-    for c in range(parts):
+    for c in range(n_parts):
         drain(noise_all.at[c, pl.ds(0, n - 1)], ns_sem.at[c])
+    for c in range(parts):
         drain(t_all.at[c, pl.ds(0, n - 1)], ts_sem.at[c])
     drain(mass_all.at[pl.ds(0, g - 1)], ms_sem)
 
@@ -186,7 +193,7 @@
     n_loc = sites.shape[0]
     rows = rows_dev * n
     lanes = max(128, rows)
-    chunks, parts = 8, 4
+    chunks, parts, n_parts = 4, 4, 2
     vmem = pl.BlockSpec(memory_space=pltpu.VMEM)
     anym = pl.BlockSpec(memory_space=pl.ANY)
     dma = pltpu.SemaphoreType.DMA
@@ -202,16 +209,16 @@
         scratch_shapes=[
             pltpu.VMEM((n_loc, width), BF16),
             pltpu.VMEM((1, n_loc), F32),
-            pltpu.VMEM((parts, n, rows_dev, width // parts), BF16),
-            pltpu.VMEM((parts, rows, width // parts), F32),
+            pltpu.VMEM((n_parts, n, rows_dev, width // n_parts), BF16),
+            pltpu.VMEM((n_parts, rows, width // n_parts), F32),
             pltpu.VMEM((n_loc, 128), F32),
             pltpu.VMEM((parts, n, rows_dev, width // parts), BF16),
             pltpu.VMEM((parts, n, rows_dev, width // parts), BF16),
-            pltpu.VMEM((1, lanes), F32),
-            pltpu.VMEM((n, 1, lanes), F32),
+            pltpu.VMEM((2, lanes), F32),
+            pltpu.VMEM((n, 2, lanes), F32),
             pltpu.VMEM((1, n_loc), F32),
             pltpu.VMEM((g, 1, n_loc), F32),
-            dma((chunks,)), dma((2,)), dma((parts,)), dma((parts,)), dma((parts,)), dma((parts,)),
+            dma((chunks,)), dma((2,)), dma((n_parts,)), dma((n_parts,)), dma((parts,)), dma((parts,)),
             dma(()), dma(()), dma(()), dma(()),
         ],
         compiler_params=pltpu.CompilerParams(

time: 20.9 us -> 21.9 us (1.048)
  Pallas kernels: 20.1 us -> 21.1 us
    pallas_call x1, Pallas kernels: 19.5 us -> 20.4 us  [shards(): pl.pallas_call(functools.partial(kernel, n, g), out_shape=(pltpu.VMEM((ro...]
where the time goes in v2:
time: 21.9 us; the launch traced here: 21.7 us
  Pallas kernels  21.1 us (96%)
  between operations  0.64 us (3%)
    pallas_call x1, Pallas kernels, shards(): pl.pallas_call(functools.partial(kernel, n, g), out_shape=(pltpu.VMEM((ro...  20.4 us
    pallas_call x1, Pallas kernels, shards(): pl.pallas_call(place, out_shape=tuple((jax.ShapeDtypeStruct(o.shape, o.dt...  0.64 us

profile of v2, /device:TPU:0, one launch (start us, length us, event | category | flops | bytes accessed | tf_op | source)
XLA Modules:
  0.0 21.7 jit_solution(8012763482680407751)
XLA Ops:
  0.6 20.4 %dual_step.1 = (bf16[2,4096]{1,0:T(2,128)(2,1)S(1)}, f32[1,2]{1,0:T(1,128)S(1)}, f32[1,512]{1,0:T(1,128)S(1)}) custom-call(bf16[2,4096]{1,0:T(2,128)(2,1)} %noise_ref.1, bf16[512,4096]{1,0:T(8,128)(2,1)} %sites_ref.1, f32[1,512]{1,0:T(1,128)} %bitcast.5), custom_call_target="tpu_custom_call" | custom-call | tf_op jit(solution)/shard_map/dual_step/pallas_call | solution.py:200
  21.1 0.6 %place.1 = (bf16[2,4096]{1,0:T(2,128)(2,1)}, f32[2]{0:T(128)}, f32[512]{0:T(512)}) custom-call(bf16[2,4096]{1,0:T(2,128)(2,1)S(1)} %get-tuple-element.6.tgt, f32[2]{0:T(128)S(1)} %bitcast.4, f32[512]{0:T(512)S(1)} %bitcast.3), custom_call_target="tpu_custom_call" | custom-call | tf_op jit(solution)/shard_map/place/pallas_call | solution.py:229

commit v3 on v0

--- a/solution.py
+++ b/solution.py
@@ -112,7 +112,7 @@
 
     probs = shifted.astype(BF16)
     inv = 1.0 / total
-    for c in range(parts):
+    def targets(c):
         part = jnp.dot(probs, sites_v[:, c * wide:(c + 1) * wide], preferred_element_type=F32) * inv
         for d in range(n):
             t_send[c, d] = part[d * rows_dev:(d + 1) * rows_dev, :].astype(BF16)
@@ -122,6 +122,9 @@
             to_site(t_send.at[c, t], t_all.at[c, me], ts_sem.at[c], tr_sem.at[c], t)
 
         steps(n - 1, t_to)
+
+    for c in range(parts // 2):
+        targets(c)
 
     drain(stat_all.at[pl.ds(0, n - 1)], sr_sem)
     stats = stat_all[...]
@@ -138,6 +141,9 @@
 
     steps(g - 1, mass_to)
     mass_all[mg] = mass_part
+
+    for c in range(parts // 2, parts):
+        targets(c)
 
     mine_diag = (lax.broadcasted_iota(jnp.int32, (rows_dev, lanes), 0) + me * rows_dev
                  == lax.broadcasted_iota(jnp.int32, (rows_dev, lanes), 1))

time: 20.9 us -> 21.6 us (1.033)
  Pallas kernels: 20.1 us -> 20.8 us
    pallas_call x1, Pallas kernels: 19.5 us -> 20.2 us  [shards(): pl.pallas_call(functools.partial(kernel, n, g), out_shape=(pltpu.VMEM((ro...]
where the time goes in v3:
time: 21.6 us; the launch traced here: 21.5 us
  Pallas kernels  20.8 us (96%)
  between operations  0.64 us (3%)
    pallas_call x1, Pallas kernels, shards(): pl.pallas_call(functools.partial(kernel, n, g), out_shape=(pltpu.VMEM((ro...  20.2 us
    pallas_call x1, Pallas kernels, shards(): pl.pallas_call(place, out_shape=tuple((jax.ShapeDtypeStruct(o.shape, o.dt...  0.64 us

profile of v3, /device:TPU:0, one launch (start us, length us, event | category | flops | bytes accessed | tf_op | source)
XLA Modules:
  0.0 21.5 jit_solution(18061915778271849806)
XLA Ops:
  0.6 20.2 %dual_step.1 = (bf16[2,4096]{1,0:T(2,128)(2,1)S(1)}, f32[1,2]{1,0:T(1,128)S(1)}, f32[1,512]{1,0:T(1,128)S(1)}) custom-call(bf16[2,4096]{1,0:T(2,128)(2,1)} %noise_ref.1, bf16[512,4096]{1,0:T(8,128)(2,1)} %sites_ref.1, f32[1,512]{1,0:T(1,128)} %bitcast.5), custom_call_target="tpu_custom_call" | custom-call | tf_op jit(solution)/shard_map/dual_step/pallas_call | solution.py:199
  20.8 0.6 %place.1 = (bf16[2,4096]{1,0:T(2,128)(2,1)}, f32[2]{0:T(128)}, f32[512]{0:T(512)}) custom-call(bf16[2,4096]{1,0:T(2,128)(2,1)S(1)} %get-tuple-element.6.tgt, f32[2]{0:T(128)S(1)} %bitcast.4, f32[512]{0:T(512)S(1)} %bitcast.3), custom_call_target="tpu_custom_call" | custom-call | tf_op jit(solution)/shard_map/place/pallas_call | solution.py:228
